TPU v7x, 256 devices: a whole 4x4x8 slice. The times are simulated.
256 devices in a mesh: sec: 8 (over y, core), xy: 32 (over z, x).
Axes of the slice: x: 4, y: 4, z: 8, core: 2. Of those that a mesh axis runs over, the one named last changes fastest.
Arguments:
- sections_img: bfloat16 [8, 8192, 2048], P('sec', 'xy'), may hold values from -8 to 8
- missing: int32 [8], replicated, may hold values 0 or 1
- patch_anchor: int32 [2, 32, 8], P(None, 'xy', 'sec'), may hold values from -64 to 64
- block_valid: int32 [32, 8], P('xy', 'sec'), may hold values 0 or 1
Outputs:
- flow: float32 [2, 2, 8, 32, 8], P(None, None, None, 'xy', 'sec')
All inputs are finite; a program needn't handle non-finite values. No bound on the sum of `block_valid` on one device may be relied on, other than what follows from the above.
Results may differ from a plain program's by a relative error of at most 0.004.
Values may be sent and summed in bfloat16 or wider, within the bound.
A program may use at most 64 MiB of HBM per device.

v0:
```python
import math

import jax
import jax.numpy as jnp
from jax import lax
from jax.sharding import PartitionSpec as P

PATCH = 256
MARGIN = 64


BETA = 30.0
SHIFT_UNIT = 8.0


def padded_2(array, sides, width):
    for axis, dim in sides:
        count, length = (lax.axis_size(axis), array.shape[dim])
        up = [(i, (i + 1) % count) for i in range(count - 1)]
        down = [(j, i) for i, j in up]
        last = lax.slice_in_dim(array, length - width, length, axis=dim)
        initial = lax.slice_in_dim(array, 0, width, axis=dim)
        before = lax.ppermute(last, axis, up)
        after = lax.ppermute(initial, axis, down)
        array = jnp.concatenate([before, array, after], axis=dim)
    return array


def dft_tables(length):
    index = jnp.arange(length, dtype=jnp.int32)
    product = index[:, None] * index[None, :] % length
    phase = product.astype(jnp.float32) * (2.0 * math.pi / length)
    return (jnp.cos(phase).astype(jnp.bfloat16), jnp.sin(phase).astype(jnp.bfloat16))


def matmul(form, left, right):
    return jnp.einsum(form, left, right, preferred_element_type=jnp.float32)


def normalize(patch):
    values = patch.astype(jnp.float32)
    centred = values - jnp.mean(values, axis=(1, 2), keepdims=True)
    spread = jnp.mean(centred * centred, axis=(1, 2), keepdims=True)
    return (centred * lax.rsqrt(spread + 1e-05)).astype(jnp.bfloat16)


def forward(normed, cosine, sine):
    first_re = matmul("npq,qk->npk", normed, cosine).astype(jnp.bfloat16)
    first_im = (-matmul("npq,qk->npk", normed, sine)).astype(jnp.bfloat16)
    spec_re = (
        matmul("jp,npk->njk", cosine, first_re) + matmul("jp,npk->njk", sine, first_im)
    ).astype(jnp.bfloat16)
    spec_im = (
        matmul("jp,npk->njk", cosine, first_im) - matmul("jp,npk->njk", sine, first_re)
    ).astype(jnp.bfloat16)
    return (spec_re, spec_im)


def correlate(left_re, left_im, right_re, right_im, cosine, sine):
    a_re = left_re.astype(jnp.float32)
    a_im = left_im.astype(jnp.float32)
    b_re = right_re.astype(jnp.float32)
    b_im = right_im.astype(jnp.float32)
    cross_re = (a_re * b_re + a_im * b_im).astype(jnp.bfloat16)
    cross_im = (a_re * b_im - a_im * b_re).astype(jnp.bfloat16)
    half_re = (
        matmul("npq,qk->npk", cross_re, cosine) - matmul("npq,qk->npk", cross_im, sine)
    ).astype(jnp.bfloat16)
    half_im = (
        matmul("npq,qk->npk", cross_re, sine) + matmul("npq,qk->npk", cross_im, cosine)
    ).astype(jnp.bfloat16)
    full = matmul("jp,npk->njk", cosine, half_re) - matmul("jp,npk->njk", sine, half_im)
    return full / float(PATCH) ** 4


def soft_shift(corr):
    length = corr.shape[1]
    index = jnp.arange(length, dtype=jnp.int32)
    signed = jnp.where(index < length // 2, index, index - length).astype(jnp.float32)
    weight = jnp.exp(BETA * corr)
    total = jnp.sum(weight, axis=(1, 2))
    shift_row = jnp.sum(weight * signed[None, :, None], axis=(1, 2)) / total / SHIFT_UNIT
    shift_col = jnp.sum(weight * signed[None, None, :], axis=(1, 2)) / total / SHIFT_UNIT
    return (shift_row, shift_col)


def block_flow(patch, present, cosine, sine):
    normed = normalize(patch)
    spec_re, spec_im = forward(normed, cosine, sine)
    per_lag = []
    for lag in (1, 2):
        corr = correlate(spec_re[:-lag], spec_im[:-lag], spec_re[lag:], spec_im[lag:], cosine, sine)
        shift_row, shift_col = soft_shift(corr)
        keep = present[:-lag] * present[lag:]
        filler = jnp.zeros((lag,), jnp.float32)
        per_lag.append(
            jnp.stack(
                [
                    jnp.concatenate([shift_row * keep, filler]),
                    jnp.concatenate([shift_col * keep, filler]),
                ]
            )
        )
    return jnp.stack(per_lag, axis=1)


def body(sections_img, missing, patch_anchor, block_valid):
    blocks = lax.all_to_all(sections_img, "sec", split_axis=2, concat_axis=0, tiled=True)
    padded = padded_2(blocks, (("sec", 2), ("xy", 1)), MARGIN)
    section_count = padded.shape[0]
    top_row = patch_anchor[0, 0, 0] + MARGIN
    left_col = patch_anchor[1, 0, 0] + MARGIN
    first_section = jnp.zeros((), jnp.int32)
    patch = lax.dynamic_slice(
        padded, (first_section, top_row, left_col), (section_count, PATCH, PATCH)
    )
    cosine, sine = dft_tables(PATCH)
    present = (1 - missing).astype(jnp.float32)

    def compute(patch_now):
        return block_flow(patch_now, present, cosine, sine)

    def skipped(patch_now):
        return jnp.zeros((2, 2, section_count), jnp.float32)

    flows = lax.cond(block_valid[0, 0] != 0, compute, skipped, patch)
    return flows[:, :, :, None, None]


def solution(mesh):
    placed = (P("sec", "xy", None), P(), P(None, "xy", "sec"), P("xy", "sec"))
    return jax.shard_map(
        body,
        mesh=mesh,
        in_specs=placed,
        out_specs=P(None, None, None, "xy", "sec"),
        check_vma=False,
    )
```

profile of v0, /device:TPU:168, one launch (start us, length us, event | category | flops | bytes accessed | tf_op | source)
XLA Modules:
  0.0 111.2 jit_solution(16759699132711089739)
XLA Ops:
  0.0 4.6 %copy.39 = bf16[1,256,2048]{1,0,2:T(2,128)(2,1)S(1)} copy(bf16[1,256,2048]{2,1,0:T(8,128)(2,1)} %param.6) | data formatting | bytes 2097152 | tf_op args[0]
  5.1 10.6 %reduce.6 = bf16[2048,256]{1,0:T(8,128)(2,1)S(1)} reduce(bf16[2048,1,256]{2,1,0:T(2,128)(2,1)S(1)} %bitcast.114, bf16[]{:T(256)} %broadcast.132), dimensions={1}, to_apply=%bitcast.87.reduce_sub_computation | reduce | bytes 2097154
  16.0 19.4 %all_to_all.18 = bf16[8,2,32768]{2,1,0:T(2,128)(2,1)S(1)} all-to-all(bf16[8,2,32768]{2,1,0:T(2,128)(2,1)S(1)} %reshape.63), channel_id=1, replica_groups=mesh['sec'=8,'xy'=32] {'sec'}, dimensions={0} | all-to-all | bytes 2097152 | tf_op jit(solution)/shard_map/all_to_all | solution.py:108
  35.4 1.0 reshape.64
  36.6 2.4 %collective-permute-start.1 = (bf16[8,256,64]{1,2,0:T(8,128)(2,1)S(1)}, bf16[8,256,64]{1,2,0:T(8,128)(2,1)S(1)}, u32[]{:S(2)}, u32[]{:S(2)}) collective-permute-start(bf16[8,256,64]{1,2,0:T(8,128)(2,1)S(1)} %get-tuple-element.212), channel_id=1, source_target_pairs={{32,0},{64,32},{96,64},{128,96},{160,128},{192,160},{224,192},{33,... | collective-permute-start | bytes 786440 | tf_op jit(solution)/shard_map/ppermute | solution.py:24
  39.1 1.9 %collective-permute-start = (bf16[8,256,64]{1,2,0:T(8,128)(2,1)S(1)}, bf16[8,256,64]{1,2,0:T(8,128)(2,1)S(1)}, u32[]{:S(2)}, u32[]{:S(2)}) collective-permute-start(bf16[8,256,64]{1,2,0:T(8,128)(2,1)S(1)} %get-tuple-element.211), channel_id=1, source_target_pairs={{0,32},{32,64},{64,96},{96,128},{128,160},{160,192},{192,224},{1,3... | collective-permute-start | bytes 786440 | tf_op jit(solution)/shard_map/ppermute | solution.py:23
  41.0 1.9 %collective-permute-done.1 = bf16[8,256,64]{1,2,0:T(8,128)(2,1)S(1)} collective-permute-done((bf16[8,256,64]{1,2,0:T(8,128)(2,1)S(1)}, bf16[8,256,64]{1,2,0:T(8,128)(2,1)S(1)}, u32[]{:S(2)}, u32[]{:S(2)}) %collective-permute-start.1) | collective-permute-done | bytes 262176 | tf_op jit(solution)/shard_map/ppermute | solution.py:24
  43.0 3.8 %collective-permute-done = bf16[8,256,64]{1,2,0:T(8,128)(2,1)S(1)} collective-permute-done((bf16[8,256,64]{1,2,0:T(8,128)(2,1)S(1)}, bf16[8,256,64]{1,2,0:T(8,128)(2,1)S(1)}, u32[]{:S(2)}, u32[]{:S(2)}) %collective-permute-start) | collective-permute-done | bytes 262176 | tf_op jit(solution)/shard_map/ppermute | solution.py:23
  47.8 5.1 %collective-permute-start.3 = (bf16[8,64,384]{2,1,0:T(8,128)(2,1)S(1)}, bf16[8,64,384]{2,1,0:T(8,128)(2,1)S(1)}, u32[]{:S(2)}, u32[]{:S(2)}) collective-permute-start(bf16[8,64,384]{2,1,0:T(8,128)(2,1)S(1)} %copy.41), channel_id=1, source_target_pairs={{1,0},{2,1},{3,2},{4,3},{5,4},{6,5},{7,6},{8,7},{9,8},{10,9},{11,1... | collective-permute-start | bytes 1179656 | tf_op jit(solution)/shard_map/ppermute | solution.py:24
  53.2 1.9 %collective-permute-start.2 = (bf16[8,64,384]{2,1,0:T(8,128)(2,1)S(1)}, bf16[8,64,384]{2,1,0:T(8,128)(2,1)S(1)}, u32[]{:S(2)}, u32[]{:S(2)}) collective-permute-start(bf16[8,64,384]{2,1,0:T(8,128)(2,1)S(1)} %copy.40), channel_id=1, source_target_pairs={{0,1},{1,2},{2,3},{3,4},{4,5},{5,6},{6,7},{7,8},{8,9},{9,10},{10,1... | collective-permute-start | bytes 1179656 | tf_op jit(solution)/shard_map/ppermute | solution.py:23
  55.8 1.7 %sine_convert_fusion = (bf16[256,256]{1,0:T(8,128)(2,1)S(1)}, bf16[256,256]{1,0:T(8,128)(2,1)}) fusion(), kind=kLoop, calls=%fused_computation.92 | loop fusion | flops 1048576 | bytes 262144 | tf_op jit(solution)/shard_map/convert_element_type | solution.py:33
  57.5 2.1 %collective-permute-done.3 = bf16[8,64,384]{2,1,0:T(8,128)(2,1)S(1)} collective-permute-done((bf16[8,64,384]{2,1,0:T(8,128)(2,1)S(1)}, bf16[8,64,384]{2,1,0:T(8,128)(2,1)S(1)}, u32[]{:S(2)}, u32[]{:S(2)}) %collective-permute-start.3) | collective-permute-done | bytes 393248 | tf_op jit(solution)/shard_map/ppermute | solution.py:24
  59.6 1.2 %copy.43 = bf16[8,64,384]{1,2,0:T(8,128)(2,1)} copy(bf16[8,64,384]{2,1,0:T(8,128)(2,1)S(1)} %collective-permute-done.3) | data formatting | bytes 786432 | tf_op jit(solution)/shard_map/ppermute | solution.py:24
  60.8 5.4 %collective-permute-done.2 = bf16[8,64,384]{2,1,0:T(8,128)(2,1)S(1)} collective-permute-done((bf16[8,64,384]{2,1,0:T(8,128)(2,1)S(1)}, bf16[8,64,384]{2,1,0:T(8,128)(2,1)S(1)}, u32[]{:S(2)}, u32[]{:S(2)}) %collective-permute-start.2) | collective-permute-done | bytes 393248 | tf_op jit(solution)/shard_map/ppermute | solution.py:23
  66.2 1.2 %copy.42 = bf16[8,64,384]{1,2,0:T(8,128)(2,1)} copy(bf16[8,64,384]{2,1,0:T(8,128)(2,1)S(1)} %collective-permute-done.2) | data formatting | bytes 786432 | tf_op jit(solution)/shard_map/ppermute | solution.py:23
  67.4 3.3 %pad_maximum_fusion.3 = bf16[8,384,384]{1,2,0:T(8,128)(2,1)S(1)} fusion(bf16[8,64,384]{1,2,0:T(8,128)(2,1)} %copy.43, bf16[8,256,64]{1,2,0:T(8,128)(2,1)} %copy-done.2, bf16[8,256,256]{1,2,0:T(8,128)(2,1)S(1)} %bitcast.112, bf16[8,256,64]{1,2,0:T(8,128)(2,1)} %copy-done.3, bf16[8,64,384]{1,2,0:T(8,128)(2,1)} %copy.42), kind=kLoop, calls=%fused_computation.84 | loop fusion | flops 11796480 | bytes 4718592 | tf_op jit(solution)/shard_map/concatenate | solution.py:25
  70.7 39.9 %conditional.1 = (f32[2,2,8,1,1]{2,1,0,4,3:T(2,128)S(1)}) conditional(s32[]{:T(128)} %bitcast.31, () %tuple.28, (s32[2,1,1]{0,2,1:T(1,128)S(1)}, bf16[8,384,384]{1,2,0:T(8,128)(2,1)S(1)}, bf16[256,256]{1,0:T(8,128)(2,1)}, bf16[256,256]{1,0:T(8,128)(2,1)}, bf16[256,256]{1,0:T(8,128)(2,1)S(1)}, /*index=5*/bf16[256,256]{1,0:T(8,128)(2,1)S(1)}, ...), branch_computations={%region_0.1_spmd, %region_1.10_spmd} | conditional | flops 4258464768 | bytes 69735464 | solution.py:126
  70.7 2.6 %copy.44 = bf16[8,384,384]{2,1,0:T(8,128)(2,1)} copy(bf16[8,384,384]{1,2,0:T(8,128)(2,1)S(1)} %get-tuple-element.169) | data formatting | bytes 4718592 | tf_op jit(solution)/shard_map
  73.4 0.6 fusion.55
  76.3 2.4 %convert_reduce_fusion = f32[8]{0:T(128)S(1)} fusion(bf16[8,384,384]{2,1,0:T(8,128)(2,1)} %copy.44, s32[]{:T(128)S(6)} %select_n.54, s32[]{:T(128)S(6)} %select_n.55), kind=kLoop, calls=%fused_computation.1 | loop fusion | flops 1048568 | bytes 1048616 | tf_op jit(solution)/shard_map/cond/branch_1_fun/reduce_sum | solution.py:42
  78.7 2.5 %fusion.2 = f32[8]{0:T(128)S(1)} fusion(f32[8]{0:T(128)S(1)} %broadcast_multiply_fusion, bf16[8,384,384]{2,1,0:T(8,128)(2,1)} %copy.44, s32[]{:T(128)S(6)} %select_n.54, s32[]{:T(128)S(6)} %select_n.55), kind=kLoop, calls=%fused_computation.8 | loop fusion | flops 2097144 | bytes 1048648 | tf_op jit(solution)/shard_map/cond/branch_1_fun/reduce_sum | solution.py:43
  81.2 2.3 %negate_convert_fusion = bf16[8,256,256]{2,1,0:T(8,128)(2,1)S(1)} fusion(bf16[256,256]{1,0:T(8,128)(2,1)S(1)} %get-tuple-element.143, f32[8]{0:T(128)S(1)} %add_rsqrt_fusion, f32[8]{0:T(128)S(1)} %broadcast_multiply_fusion, bf16[8,384,384]{2,1,0:T(8,128)(2,1)} %copy.44, s32[]{:T(128)S(6)} %select_n.54, s32[]{:T(128)S(6)} %select_n.55), kind=kOutput, calls=%fused_computation.12 | convolution fusion | flops 271581184 | bytes 2228296 | tf_op jit(solution)/shard_map/cond/branch_1_fun/npq,qk->npk/dot_general | solution.py:37
  84.0 2.3 %convolution_convert_fusion = bf16[8,256,256]{2,1,0:T(8,128)(2,1)S(1)} fusion(bf16[256,256]{1,0:T(8,128)(2,1)S(1)} %copy-done, f32[8]{0:T(128)S(1)} %add_rsqrt_fusion, f32[8]{0:T(128)S(1)} %broadcast_multiply_fusion, bf16[8,384,384]{2,1,0:T(8,128)(2,1)} %copy.44, s32[]{:T(128)S(6)} %select_n.54, s32[]{:T(128)S(6)} %select_n.55), kind=kOutput, calls=%fused_computation.35 | convolution fusion | flops 271056896 | bytes 2228296 | tf_op jit(solution)/shard_map/cond/branch_1_fun/npq,qk->npk/dot_general | solution.py:37
  87.8 1.4 %fusion.11 = (bf16[6,256,256]{1,2,0:T(8,128)(2,1)}, bf16[6,256,256]{1,2,0:T(8,128)(2,1)S(1)}) fusion(bf16[8,256,256]{1,2,0:T(8,128)(2,1)S(1)} %fusion.13, bf16[8,256,256]{1,2,0:T(8,128)(2,1)S(1)} %fusion.12), kind=kLoop, calls=%fused_computation.29 | loop fusion | flops 4718592 | bytes 4718592 | tf_op jit(solution)/shard_map/cond/branch_1_fun/convert_element_type | solution.py:65
  89.2 1.6 %fusion.24 = f32[6,256,256]{2,1,0:T(8,128)} fusion(bf16[6,256,256]{1,2,0:T(8,128)(2,1)S(1)} %get-tuple-element.198, bf16[256,256]{1,0:T(8,128)(2,1)S(1)} %copy-done), kind=kOutput, calls=%fused_computation.46 | convolution fusion | flops 201326592 | bytes 2490368 | tf_op jit(solution)/shard_map/cond/branch_1_fun/npq,qk->npk/dot_general | solution.py:37
  90.8 3.8 %fusion.15 = f32[6,256,256]{2,1,0:T(8,128)} fusion(f32[6,256,256]{2,1,0:T(8,128)} %fusion.24, bf16[6,256,256]{1,2,0:T(8,128)(2,1)} %get-tuple-element.197, bf16[256,256]{1,0:T(8,128)(2,1)S(1)} %copy-done, bf16[256,256]{1,0:T(8,128)(2,1)S(1)} %get-tuple-element.143), kind=kOutput, calls=%fused_computation.39 | convolution fusion | flops 403439616 | bytes 4194304 | tf_op jit(solution)/shard_map/cond/branch_1_fun/jp,npk->njk/dot_general | solution.py:37
  94.6 1.6 %fusion.19 = f32[6,256,256]{2,1,0:T(8,128)} fusion(bf16[6,256,256]{1,2,0:T(8,128)(2,1)S(1)} %get-tuple-element.198, bf16[256,256]{1,0:T(8,128)(2,1)S(1)} %get-tuple-element.143), kind=kOutput, calls=%fused_computation.42 | convolution fusion | flops 201326592 | bytes 2490368 | tf_op jit(solution)/shard_map/cond/branch_1_fun/npq,qk->npk/dot_general | solution.py:37
  96.1 3.3 %multiply_reduce_fusion.3 = (f32[6]{0:T(128)S(1)}, f32[6]{0:T(128)S(1)}, f32[6]{0:T(128)S(1)}) fusion(f32[256]{0:T(256)S(1)} %fusion.44, f32[6,256,256]{2,1,0:T(8,128)} %fusion.15, bf16[256,256]{1,0:T(8,128)(2,1)S(1)} %get-tuple-element.143, f32[6,256,256]{2,1,0:T(8,128)} %fusion.19, bf16[6,256,256]{1,2,0:T(8,128)(2,1)} %get-tuple-element.197, ...), kind=kOutput, calls=%fused_computation.31 | convolution fusion | flops 406192128 | bytes 4195400 | tf_op jit(solution)/shard_map/cond/branch_1_fun/jp,npk->njk/dot_general | solution.py:37
  99.6 1.5 %fusion.7 = (bf16[7,256,256]{1,2,0:T(8,128)(2,1)}, bf16[7,256,256]{1,2,0:T(8,128)(2,1)S(1)}) fusion(bf16[8,256,256]{1,2,0:T(8,128)(2,1)S(1)} %fusion.13, bf16[8,256,256]{1,2,0:T(8,128)(2,1)S(1)} %fusion.12), kind=kLoop, calls=%fused_computation.20 | loop fusion | flops 5505024 | bytes 5505024 | tf_op jit(solution)/shard_map/cond/branch_1_fun/convert_element_type | solution.py:65
  101.5 3.6 %fusion.14 = f32[7,256,256]{2,1,0:T(8,128)} fusion(f32[7,256,256]{2,1,0:T(8,128)S(1)} %fusion.34, bf16[7,256,256]{1,2,0:T(8,128)(2,1)} %get-tuple-element.195, bf16[256,256]{1,0:T(8,128)(2,1)S(1)} %copy-done, bf16[256,256]{1,0:T(8,128)(2,1)S(1)} %get-tuple-element.143), kind=kOutput, calls=%fused_computation.38 | convolution fusion | flops 470679552 | bytes 4849664 | tf_op jit(solution)/shard_map/cond/branch_1_fun/jp,npk->njk/dot_general | solution.py:37
  105.1 1.7 %fusion.29 = f32[7,256,256]{2,1,0:T(8,128)} fusion(bf16[7,256,256]{1,2,0:T(8,128)(2,1)S(1)} %get-tuple-element.196, bf16[256,256]{1,0:T(8,128)(2,1)S(1)} %get-tuple-element.143), kind=kOutput, calls=%fused_computation.50 | convolution fusion | flops 234881024 | bytes 2883584 | tf_op jit(solution)/shard_map/cond/branch_1_fun/npq,qk->npk/dot_general | solution.py:37
  106.8 3.4 %multiply_reduce_fusion.1 = (f32[7]{0:T(128)S(1)}, f32[7]{0:T(128)S(1)}, f32[7]{0:T(128)S(1)}) fusion(f32[256]{0:T(256)S(1)} %fusion.44, f32[7,256,256]{2,1,0:T(8,128)} %fusion.14, bf16[256,256]{1,0:T(8,128)(2,1)S(1)} %get-tuple-element.143, f32[7,256,256]{2,1,0:T(8,128)} %fusion.29, bf16[7,256,256]{1,2,0:T(8,128)(2,1)S(1)} %copy-done.1, ...), kind=kOutput, calls=%fused_computation.22 | convolution fusion | flops 473890816 | bytes 4850772 | tf_op jit(solution)/shard_map/cond/branch_1_fun/jp,npk->njk/dot_general | solution.py:37
  (39 shorter events, 5.6 us)
Async XLA Ops:
  36.6 6.3 %collective-permute-start.1 = (bf16[8,256,64]{1,2,0:T(8,128)(2,1)S(1)}, bf16[8,256,64]{1,2,0:T(8,128)(2,1)S(1)}, u32[]{:S(2)}, u32[]{:S(2)}) collective-permute-start(bf16[8,256,64]{1,2,0:T(8,128)(2,1)S(1)} %get-tuple-element.212), channel_id=1, source_target_pairs={{32,0},{64,32},{96,64},{128,96},{160,128},{192,160},{224,192},{33,... | collective-permute-start | bytes 786440 | tf_op jit(solution)/shard_map/ppermute | solution.py:24
  39.1 7.7 %collective-permute-start = (bf16[8,256,64]{1,2,0:T(8,128)(2,1)S(1)}, bf16[8,256,64]{1,2,0:T(8,128)(2,1)S(1)}, u32[]{:S(2)}, u32[]{:S(2)}) collective-permute-start(bf16[8,256,64]{1,2,0:T(8,128)(2,1)S(1)} %get-tuple-element.211), channel_id=1, source_target_pairs={{0,32},{32,64},{64,96},{96,128},{128,160},{160,192},{192,224},{1,3... | collective-permute-start | bytes 786440 | tf_op jit(solution)/shard_map/ppermute | solution.py:23
  43.0 4.3 %copy-start.2 = (bf16[8,256,64]{1,2,0:T(8,128)(2,1)}, bf16[8,256,64]{1,2,0:T(8,128)(2,1)S(1)}, u32[]{:S(2)}) copy-start(bf16[8,256,64]{1,2,0:T(8,128)(2,1)S(1)} %collective-permute-done.1) | copy-start | bytes 786436
  46.8 0.7 copy-start.3
  47.5 10.0 %copy-start.6 = (s32[8]{0:T(128)S(1)}, s32[8]{0:T(128)}, u32[]{:S(2)}) copy-start(s32[8]{0:T(128)} %param.7) | copy-start | bytes 100
  47.8 11.8 %collective-permute-start.3 = (bf16[8,64,384]{2,1,0:T(8,128)(2,1)S(1)}, bf16[8,64,384]{2,1,0:T(8,128)(2,1)S(1)}, u32[]{:S(2)}, u32[]{:S(2)}) collective-permute-start(bf16[8,64,384]{2,1,0:T(8,128)(2,1)S(1)} %copy.41), channel_id=1, source_target_pairs={{1,0},{2,1},{3,2},{4,3},{5,4},{6,5},{7,6},{8,7},{9,8},{10,9},{11,1... | collective-permute-start | bytes 1179656 | tf_op jit(solution)/shard_map/ppermute | solution.py:24
  53.2 12.9 %collective-permute-start.2 = (bf16[8,64,384]{2,1,0:T(8,128)(2,1)S(1)}, bf16[8,64,384]{2,1,0:T(8,128)(2,1)S(1)}, u32[]{:S(2)}, u32[]{:S(2)}) collective-permute-start(bf16[8,64,384]{2,1,0:T(8,128)(2,1)S(1)} %copy.40), channel_id=1, source_target_pairs={{0,1},{1,2},{2,3},{3,4},{4,5},{5,6},{6,7},{7,8},{8,9},{9,10},{10,1... | collective-permute-start | bytes 1179656 | tf_op jit(solution)/shard_map/ppermute | solution.py:23
  67.4 3.3 %copy-start.5 = (s32[2,1,1]{0,2,1:T(1,128)S(1)}, s32[2,1,1]{0,2,1:T(1,128)}, u32[]{:S(2)}) copy-start(s32[2,1,1]{0,2,1:T(1,128)} %param.8) | copy-start | bytes 28
  78.7 4.9 %copy-start = (bf16[256,256]{1,0:T(8,128)(2,1)S(1)}, bf16[256,256]{1,0:T(8,128)(2,1)}, u32[]{:S(2)}) copy-start(bf16[256,256]{1,0:T(8,128)(2,1)} %get-tuple-element.142) | copy-start | bytes 393220 | tf_op jit(solution)/shard_map/cond
  105.1 1.7 %copy-start.1 = (bf16[7,256,256]{1,2,0:T(8,128)(2,1)S(1)}, bf16[7,256,256]{1,2,0:T(8,128)(2,1)}, u32[]{:S(2)}) copy-start(bf16[7,256,256]{1,2,0:T(8,128)(2,1)} %get-tuple-element.195) | copy-start | bytes 2752516 | tf_op jit(solution)/shard_map/cond
  110.6 0.6 copy-start.4
where the time goes:
time: 112 us; the launch traced here: 111 us
  matrix products  25.9 us (23%)
  other arithmetic  23.8 us (21%)
  blocking collectives  19.4 us (17%)
  local copies, waits for them, and re-layouts  14 us (12%)
  waiting for transfers between devices  13.2 us (12%)
  starting transfers between devices  11.4 us (10%)
  loops' own time  2.69 us (2%)
    dot_general x14, matrix products, matmul(): return jnp.einsum(form, left, right, preferred_element_type=jnp.float32)  25.9 us
    all_to_all x1, blocking collectives, body(): lax.all_to_all(sections_img, 'sec', split_axis=2, concat_axis=0, tiled=True)  19.4 us
    unnamed x1, other arithmetic  10.6 us
    ppermute x2, waiting for transfers between devices, padded_2(): before = lax.ppermute(last, axis, up)  9.19 us
    ppermute x2, starting transfers between devices, padded_2(): after = lax.ppermute(initial, axis, down)  7.56 us
    unnamed x15, local copies, waits for them, and re-layouts  7.41 us
    ppermute x2, waiting for transfers between devices, padded_2(): after = lax.ppermute(initial, axis, down)  4.06 us
    ppermute x2, starting transfers between devices, padded_2(): before = lax.ppermute(last, axis, up)  3.84 us
  transfers between devices with their start and end apart: 4, of which 4 were waited for; matrix products, arithmetic and copies ran while one was open for 3% of the time, Pallas kernels for 0%

commit v1 on v0

v1 whole, which is shorter than its diff:
```python
import functools
import math

import jax
import jax.numpy as jnp
import numpy as np
from jax import lax
from jax.experimental import pallas as pl
from jax.experimental.pallas import tpu as pltpu
from jax.sharding import PartitionSpec as P

PATCH = 256
HALF = PATCH // 2
MARGIN = 64
LANES = 128
EXTRA = 16
BETA = 30.0
SHIFT_UNIT = 8.0
MESH = pl.DeviceIdType.MESH


def tables():
    index = np.arange(PATCH)
    phase = (index[:, None] * index[None, :] % PATCH).astype(np.float32) * np.float32(2.0 * math.pi / PATCH)
    cosine, sine = np.cos(phase), np.sin(phase)
    alternating = np.where(index % 2 == 0, 1.0, -1.0).astype(np.float32)
    analysis = np.concatenate([cosine[:HALF], -sine[:HALF]], axis=0)
    analysis[HALF] = alternating
    synthesis = np.concatenate([2.0 * cosine[:, :HALF], -2.0 * sine[:, :HALF]], axis=1)
    synthesis[:, 0] = 1.0
    synthesis[:, HALF] = alternating
    return np.stack([cosine, sine, analysis, synthesis]).astype(jnp.bfloat16)


def dot(left, right):
    return jnp.dot(left, right, preferred_element_type=jnp.float32)


def kernel(
    sec_count,
    row_count,
    x_ref,
    anchor_ref,
    table_ref,
    out_ref,
    own,
    above,
    below,
    table,
    anchors,
    patch,
    send,
    spec,
    stat_plain,
    stat_row,
    local_sem,
    halo_send,
    halo_recv,
    anchor_send,
    anchor_recv,
    spec_send,
    spec_recv,
):
    a = lax.axis_index("sec")
    r = lax.axis_index("xy")
    row_next = lax.rem(r + 1, row_count)
    row_before = lax.rem(r + row_count - 1, row_count)
    wide = sec_count * PATCH

    local_own = pltpu.make_async_copy(x_ref.at[0], own.at[:, pl.ds(LANES, wide)], local_sem.at[0])
    local_table = pltpu.make_async_copy(table_ref, table, local_sem.at[1])
    local_own.start()
    local_table.start()

    barrier = pltpu.get_barrier_semaphore()
    for other in (row_next, row_before):
        pl.semaphore_signal(barrier, inc=1, device_id=(a, other), device_id_type=MESH)
    for step in range(1, sec_count):
        pl.semaphore_signal(barrier, inc=1, device_id=(lax.rem(a + step, sec_count), r), device_id_type=MESH)

    me_row = jnp.full((1, LANES), anchor_ref[0, 0, 0], jnp.float32)
    me_col = jnp.full((1, LANES), anchor_ref[1, 0, 0], jnp.float32)
    anchors[a] = jnp.concatenate([me_row, me_col, jnp.zeros((6, LANES), jnp.float32)], axis=0)
    for ref in (own, above, below):
        rows = ref.shape[0]
        ref[:, 0:LANES] = jnp.zeros((rows, LANES), jnp.bfloat16)
        ref[:, LANES + wide :] = jnp.zeros((rows, LANES), jnp.bfloat16)
    stat_plain[...] = jnp.ones_like(stat_plain)
    stat_row[...] = jnp.zeros_like(stat_row)

    pl.semaphore_wait(barrier, sec_count + 1)

    def anchor_copy(step):
        to = lax.rem(a + step, sec_count)
        return pltpu.make_async_remote_copy(
            src_ref=anchors.at[a],
            dst_ref=anchors.at[a],
            send_sem=anchor_send.at[step],
            recv_sem=anchor_recv.at[step],
            device_id=(to, r),
            device_id_type=MESH,
        )

    first = lax.rem(a + 2, sec_count)

    def halo_copy(step, side):
        at = lax.rem(first + step + sec_count - 1, sec_count)
        source = pl.ds(pl.multiple_of(at * PATCH, PATCH), PATCH)
        target = pl.ds(pl.multiple_of(at * PATCH + LANES, LANES), PATCH)
        rows, ref, to = ((PATCH - MARGIN, above, row_next), (0, below, row_before))[side]
        return pltpu.make_async_remote_copy(
            src_ref=x_ref.at[0, pl.ds(rows, MARGIN), source],
            dst_ref=ref.at[:, target],
            send_sem=halo_send.at[side, step],
            recv_sem=halo_recv.at[side, step],
            device_id=(a, to),
            device_id_type=MESH,
        )

    for step in range(1, sec_count):
        anchor_copy(step).start()
    for step in range(sec_count):
        for side in (0, 1):
            halo_copy(step, side).start()

    local_own.wait()
    local_table.wait()
    for step in range(1, sec_count):
        anchor_copy(step).wait_recv()

    def spec_copy(step):
        to = lax.rem(first + step, sec_count)
        return pltpu.make_async_remote_copy(
            src_ref=send.at[step],
            dst_ref=spec.at[a],
            send_sem=spec_send.at[step],
            recv_sem=spec_recv.at[a],
            device_id=(to, r),
            device_id_type=MESH,
        )

    def wait_halo(step):
        for side in (0, 1):
            halo_copy(step, side).wait_recv()

    wait_halo(0)
    wait_halo(1)
    has_next = jnp.where(r < row_count - 1, 1.0, 0.0)
    has_before = jnp.where(r > 0, 1.0, 0.0)

    def transform(step, _):
        @pl.when(step < sec_count - 2)
        def _():
            wait_halo(step + 2)

        c = lax.rem(first + step, sec_count)
        base = pl.multiple_of(c * PATCH + LANES, LANES)
        shift_row = anchors[c, 0:1, :]
        shift_col = anchors[c, 1:2, :]

        def rows_of(offset):
            lanes = pl.ds(pl.multiple_of(base + offset, LANES), LANES)
            sub = lax.broadcasted_iota(jnp.int32, (MARGIN, LANES), 0).astype(jnp.float32)
            top = jnp.where(
                sub < shift_row,
                below[:, lanes].astype(jnp.float32) * has_next,
                own[0:MARGIN, lanes].astype(jnp.float32),
            )
            middle = own[MARGIN : PATCH - MARGIN, lanes].astype(jnp.float32)
            bottom = jnp.where(
                sub >= shift_row + MARGIN,
                above[:, lanes].astype(jnp.float32) * has_before,
                own[PATCH - MARGIN :, lanes].astype(jnp.float32),
            )
            return jnp.concatenate([top, middle, bottom], axis=0)

        lane = lax.broadcasted_iota(jnp.int32, (PATCH, LANES), 1).astype(jnp.float32)
        left = jnp.where(lane < shift_col, rows_of(PATCH), rows_of(0))
        right = jnp.where(lane >= shift_col + LANES, rows_of(-LANES), rows_of(LANES))
        patch[:, 0:LANES] = left
        patch[:, LANES:] = right
        values = patch[...]
        count = 1.0 / (PATCH * PATCH)
        centred = values - jnp.sum(values) * count
        spread = jnp.sum(centred * centred) * count
        normed = (centred * lax.rsqrt(jnp.full((1, 1), spread + 1e-05, jnp.float32))).astype(jnp.bfloat16)

        rows = dot(table[2], normed).astype(jnp.bfloat16)
        by_cos = dot(rows, table[0])
        by_sin = dot(rows, table[1])
        head = lax.broadcasted_iota(jnp.int32, (HALF, PATCH), 0) == 0
        zero = jnp.zeros((HALF, PATCH), jnp.float32)
        spec_re = by_cos[:HALF] + jnp.where(head, zero, by_sin[HALF:])
        spec_im = jnp.where(head, zero, by_cos[HALF:]) - by_sin[:HALF]
        last_re = jnp.where(head, by_cos[HALF:], zero)[:8]
        last_im = jnp.where(head, -by_sin[HALF:], zero)[:8]
        send[step, 0:HALF, :] = spec_re.astype(jnp.bfloat16)
        send[step, HALF:PATCH, :] = spec_im.astype(jnp.bfloat16)
        send[step, PATCH:, :] = jnp.concatenate([last_re, last_im], axis=0).astype(jnp.bfloat16)

        @pl.when(c != a)
        def _():
            spec_copy(step).start()

        @pl.when(c == a)
        def _():
            spec[a] = send[step]

        return 0

    lax.fori_loop(0, sec_count, transform, 0)

    def arrived(s):
        @pl.when(s != a)
        def _():
            pltpu.make_async_remote_copy(
                src_ref=send.at[0],
                dst_ref=spec.at[s],
                send_sem=spec_send.at[0],
                recv_sem=spec_recv.at[s],
                device_id=(s, r),
                device_id_type=MESH,
            ).wait_recv()

    def cross(s, t):
        a_re = spec[s, 0:HALF, :].astype(jnp.float32)
        a_im = spec[s, HALF:PATCH, :].astype(jnp.float32)
        b_re = spec[t, 0:HALF, :].astype(jnp.float32)
        b_im = spec[t, HALF:PATCH, :].astype(jnp.float32)
        cross_re = a_re * b_re + a_im * b_im
        cross_im = a_re * b_im - a_im * b_re
        e = spec[s, PATCH:, :].astype(jnp.float32)
        f = spec[t, PATCH:, :].astype(jnp.float32)
        last_re = e[:8] * f[:8] + e[8:] * f[8:]
        last_im = e[:8] * f[8:] - e[8:] * f[:8]
        cross_re = jnp.concatenate([cross_re[:8] - last_im, cross_re[8:]], axis=0)
        cross_im = jnp.concatenate([cross_im[:8] + last_re, cross_im[8:]], axis=0)
        return jnp.concatenate([cross_re, cross_im], axis=0).astype(jnp.bfloat16)

    scale = BETA / math.log(2.0) / float(PATCH) ** 4
    group = lax.broadcasted_iota(jnp.int32, (PATCH // 8, 8, PATCH), 0).astype(jnp.float32) * 8.0
    signed_group = jnp.where(group < HALF, group, group - PATCH)

    def correlate(s, t, slot):
        pair = cross(s, t)
        by_cos = dot(pair, table[0])
        by_sin = dot(pair, table[1])
        half_re = by_cos[:HALF] - by_sin[HALF:]
        half_im = by_sin[:HALF] + by_cos[HALF:]
        half = jnp.concatenate([half_re, half_im], axis=0).astype(jnp.bfloat16)
        weight = jnp.exp2(dot(table[3], half) * scale).reshape(PATCH // 8, 8, PATCH)
        stat_plain[slot] = jnp.sum(weight, axis=0)
        stat_row[slot] = jnp.sum(weight * signed_group, axis=0)

    arrived(0)

    def pairs(t, _):
        arrived(t)
        correlate(t - 1, t, t - 1)
        back = jnp.maximum(t - 2, 0)
        correlate(back, t, jnp.where(t >= 2, sec_count + back, 2 * sec_count - 1))
        return 0

    lax.fori_loop(1, sec_count, pairs, 0)

    plain = stat_plain[...]
    sub = lax.broadcasted_iota(jnp.int32, plain.shape, 1).astype(jnp.float32)
    by_row = jnp.sum(stat_row[...] + sub * plain, axis=1)
    plain = jnp.sum(plain, axis=1)
    column = lax.broadcasted_iota(jnp.int32, plain.shape, 1).astype(jnp.float32)
    signed = jnp.where(column < HALF, column, column - PATCH)
    total = jnp.sum(plain, axis=1, keepdims=True)
    shift_row = jnp.sum(by_row, axis=1, keepdims=True) / total / SHIFT_UNIT
    shift_col = jnp.sum(plain * signed, axis=1, keepdims=True) / total / SHIFT_UNIT
    lane = lax.broadcasted_iota(jnp.int32, out_ref.shape, 1)
    out_ref[...] = jnp.where(lane == 0, shift_row, shift_col)

    for step in range(1, sec_count):
        anchor_copy(step).wait_send()
    for step in range(sec_count):
        for side in (0, 1):
            halo_copy(step, side).wait_send()

    def sent(step, _):
        @pl.when(lax.rem(first + step, sec_count) != a)
        def _():
            spec_copy(step).wait_send()

        return 0

    lax.fori_loop(0, sec_count, sent, 0)


def body(sec_count, row_count, sections_img, missing, patch_anchor, block_valid):
    wide = sec_count * PATCH
    bf16, f32 = jnp.bfloat16, jnp.float32
    dma = pltpu.SemaphoreType.DMA
    shifts = pl.pallas_call(
        functools.partial(kernel, sec_count, row_count),
        out_shape=jax.ShapeDtypeStruct((2 * sec_count, LANES), f32),
        in_specs=[
            pl.BlockSpec(memory_space=pl.ANY),
            pl.BlockSpec(memory_space=pltpu.SMEM),
            pl.BlockSpec(memory_space=pl.ANY),
        ],
        out_specs=pl.BlockSpec(memory_space=pltpu.VMEM),
        scratch_shapes=[
            pltpu.VMEM((PATCH, wide + 2 * LANES), bf16),
            pltpu.VMEM((MARGIN, wide + 2 * LANES), bf16),
            pltpu.VMEM((MARGIN, wide + 2 * LANES), bf16),
            pltpu.VMEM((4, PATCH, PATCH), bf16),
            pltpu.VMEM((sec_count, 8, LANES), f32),
            pltpu.VMEM((PATCH, PATCH), f32),
            pltpu.VMEM((sec_count, PATCH + EXTRA, PATCH), bf16),
            pltpu.VMEM((sec_count, PATCH + EXTRA, PATCH), bf16),
            pltpu.VMEM((2 * sec_count, 8, PATCH), f32),
            pltpu.VMEM((2 * sec_count, 8, PATCH), f32),
            dma((2,)),
            dma((2, sec_count)),
            dma((2, sec_count)),
            dma((sec_count,)),
            dma((sec_count,)),
            dma((sec_count,)),
            dma((sec_count,)),
        ],
        compiler_params=pltpu.CompilerParams(
            collective_id=0, has_side_effects=True, vmem_limit_bytes=40 * 2**20
        ),
        name="flow",
    )(sections_img, patch_anchor, jnp.asarray(tables()))
    present = (1 - missing).astype(f32)
    valid = block_valid[0, 0].astype(f32)
    moved = jnp.transpose(shifts[:, :2].reshape(2, sec_count, 2), (2, 0, 1))
    keep = []
    for lag in (1, 2):
        both = present[:-lag] * present[lag:] * valid
        keep.append(jnp.concatenate([both, jnp.zeros((lag,), f32)]))
    return (moved * jnp.stack(keep)[None])[:, :, :, None, None]


def solution(mesh):
    placed = (P("sec", "xy", None), P(), P(None, "xy", "sec"), P("xy", "sec"))
    return jax.shard_map(
        functools.partial(body, mesh.shape["sec"], mesh.shape["xy"]),
        mesh=mesh,
        in_specs=placed,
        out_specs=P(None, None, None, "xy", "sec"),
        check_vma=False,
    )
```

time: 112 us -> 41.9 us (0.37)
  the two profiles are of different devices: /device:TPU:168 before, /device:TPU:1 now
where the time goes in v1:
time: 41.9 us; the launch traced here: 41.8 us
  Pallas kernels  36.6 us (87%)
  local copies, waits for them, and re-layouts  3.66 us (9%)
  other arithmetic  0.82 us (2%)
  between operations  0.68 us (2%)
    pallas_call x1, Pallas kernels, body(): pl.pallas_call(functools.partial(kernel, sec_count, row_count), out_shape...  36.6 us
    unnamed x7, local copies, waits for them, and re-layouts  3.57 us

profile of v1, /device:TPU:1, one launch (start us, length us, event | category | flops | bytes accessed | tf_op | source)
XLA Modules:
  0.0 41.8 jit_solution(13527322244964997939)
XLA Ops:
  0.0 0.7 %copy.6.anchor_ref = s32[2,1,1]{2,1,0:T(1,128)S(1)} copy(s32[2,1,1]{0,2,1:T(1,128)} %param.7) | data formatting | bytes 16 | tf_op args[2]
  0.7 0.0 copy-start
  0.7 1.2 %copy-done = bf16[1,256,2048]{2,1,0:T(8,128)(2,1)S(1)} copy-done((bf16[1,256,2048]{2,1,0:T(8,128)(2,1)S(1)}, bf16[1,256,2048]{2,1,0:T(8,128)(2,1)}, u32[]{:S(2)}) %copy-start) | copy-done | bytes 1048600
  2.0 0.0 copy-start.1
  2.0 1.0 %copy-done.1 = bf16[4,256,256]{2,1,0:T(8,128)(2,1)S(1)} copy-done((bf16[4,256,256]{2,1,0:T(8,128)(2,1)S(1)}, bf16[4,256,256]{2,1,0:T(8,128)(2,1)}, u32[]{:S(2)}) %copy-start.1) | copy-done | bytes 524312
  3.0 36.6 %flow.1 = f32[16,128]{1,0:T(8,128)S(1)} custom-call(bf16[1,256,2048]{2,1,0:T(8,128)(2,1)S(1)} %copy-done, s32[2,1,1]{2,1,0:T(1,128)S(1)} %copy.6.anchor_ref, bf16[4,256,256]{2,1,0:T(8,128)(2,1)S(1)} %copy-done.1), custom_call_target="tpu_custom_call" | custom-call | tf_op jit(solution)/shard_map/flow/pallas_call | solution.py:298
  39.6 0.0 copy-start.2
  39.6 0.1 copy.9
  39.7 0.6 %copy-done.2 = s32[8]{0:T(128)S(1)} copy-done((s32[8]{0:T(128)S(1)}, s32[8]{0:T(128)}, u32[]{:S(2)}) %copy-start.2) | copy-done | bytes 56
  40.9 0.1 multiply_multiply_fusion.1
  41.0 0.1 multiply_multiply_fusion
  41.1 0.1 maximum_bitcast_fusion
  41.2 0.6 %broadcast_multiply_fusion = f32[2,8,2]{1,0,2:T(2,128)} fusion(f32[2,8,2]{1,0,2:T(2,128)S(1)} %copy.9, f32[2,8]{1,0:T(2,128)S(1)} %pad_maximum_fusion), kind=kLoop, calls=%fused_computation.2 | loop fusion | flops 32 | bytes 320 | tf_op jit(solution)/shard_map/mul | solution.py:338
  (3 shorter events, 0.0 us)
Async XLA Ops:
  0.7 1.2 %copy-start = (bf16[1,256,2048]{2,1,0:T(8,128)(2,1)S(1)}, bf16[1,256,2048]{2,1,0:T(8,128)(2,1)}, u32[]{:S(2)}) copy-start(bf16[1,256,2048]{2,1,0:T(8,128)(2,1)} %x_ref.1) | copy-start | bytes 3145732
  2.0 1.0 %copy-start.1 = (bf16[4,256,256]{2,1,0:T(8,128)(2,1)S(1)}, bf16[4,256,256]{2,1,0:T(8,128)(2,1)}, u32[]{:S(2)}) copy-start(bf16[4,256,256]{2,1,0:T(8,128)(2,1)} %constant.8.clone.table_ref) | copy-start | bytes 1572868
  39.6 0.7 %copy-start.2 = (s32[8]{0:T(128)S(1)}, s32[8]{0:T(128)}, u32[]{:S(2)}) copy-start(s32[8]{0:T(128)} %param.6) | copy-start | bytes 100

commit v2 on v0

v2 whole, which is shorter than its diff:
```python
import functools
import math

import jax
import jax.numpy as jnp
import numpy as np
from jax import lax
from jax.experimental import pallas as pl
from jax.experimental.pallas import tpu as pltpu
from jax.sharding import PartitionSpec as P

PATCH = 256
HALF = PATCH // 2
MARGIN = 64
LANES = 128
EXTRA = 16
SECTIONS = 8
CHIPS = 4
BETA = 30.0
SHIFT_UNIT = 8.0
MESH = pl.DeviceIdType.MESH


def tables():
    index = np.arange(PATCH)
    phase = (index[:, None] * index[None, :] % PATCH).astype(np.float32) * np.float32(2.0 * math.pi / PATCH)
    cosine, sine = np.cos(phase), np.sin(phase)
    alternating = np.where(index % 2 == 0, 1.0, -1.0).astype(np.float32)
    analysis = np.concatenate([cosine[:HALF], -sine[:HALF]], axis=0)
    analysis[HALF] = alternating
    synthesis = np.concatenate([2.0 * cosine[:, :HALF], -2.0 * sine[:, :HALF]], axis=1)
    synthesis[:, 0] = 1.0
    synthesis[:, HALF] = alternating
    return np.stack([cosine, sine, analysis, synthesis]).astype(jnp.bfloat16)


def dot(left, right):
    return jnp.dot(left, right, preferred_element_type=jnp.float32)


def plan():
    orders = []
    for a in range(SECTIONS):
        y, k = a // 2, a % 2
        sign = 1 - 2 * k
        same = [2 * ((y - sign * j) % CHIPS) + k for j in range(CHIPS)]
        peer = [2 * ((y + sign * j) % CHIPS) + 1 - k for j in range(CHIPS)]
        orders.append(same + [peer[1], peer[0], peer[2], peer[3]])
    pairs = range(2 * SECTIONS - 3)
    ready = []
    for order in orders:
        rank = {s: i for i, s in enumerate(order)}
        ready.append(sorted((max(rank[n // 2], rank[n // 2 + 1 + n % 2]), n) for n in pairs))
    steps = [max(entry[i][0] for entry in ready) for i in range(len(pairs))]
    waits = [tuple(order[i] for order in orders) for i in range(SECTIONS)]
    work = [[tuple(entry[i][1] for entry in ready) for i in range(len(pairs)) if steps[i] == q] for q in range(SECTIONS)]
    return waits, work


def pick(values, a):
    if max(values) < 8:
        power = (1 + 7 * (a % 2)) * (1 + 63 * (a // 2 % 2)) * (1 + 4095 * (a // 4))
        return sum(v * 8**i for i, v in enumerate(values)) // power % 8
    return 8 * pick([v // 8 for v in values], a) + pick([v % 8 for v in values], a)


def kernel(
    row_count,
    x_ref,
    anchor_ref,
    missing_ref,
    valid_ref,
    table_ref,
    out_ref,
    anchor,
    missing,
    valid,
    own,
    above,
    below,
    table,
    anchors,
    send,
    passing,
    spec,
    stat_plain,
    stat_row,
    local_sem,
    halo_send,
    halo_recv,
    anchor_send,
    anchor_recv,
    spec_send,
    spec_recv,
    passing_recv,
    passing_send,
):
    a = lax.axis_index("sec")
    r = lax.axis_index("xy")
    y, k = a // 2, a % 2
    sign = 1 - 2 * k
    peer = a + sign
    has_next = 1 - (r + 1) // row_count
    has_before = (r + row_count - 1) // row_count
    wide = SECTIONS * PATCH

    def chip(j):
        return (y + sign * j + 2 * CHIPS) % CHIPS

    def local(source, target, i):
        return pltpu.make_async_copy(source, target, local_sem.at[i])

    def remote(source, target, sent, received, to_a, to_r):
        return pltpu.make_async_remote_copy(
            src_ref=source,
            dst_ref=target,
            send_sem=sent,
            recv_sem=received,
            device_id=(to_a, to_r),
            device_id_type=MESH,
        )

    local_own = local(x_ref.at[0], own.at[:, pl.ds(LANES, wide)], 0)
    local_table = local(table_ref, table, 1)
    small = [local(anchor_ref, anchor, 2), local(missing_ref, missing, 3), local(valid_ref, valid, 4)]
    for copy in small:
        copy.start()
    local_own.start()
    local_table.start()

    barrier = pltpu.get_barrier_semaphore()

    @pl.when(has_next == 1)
    def _():
        pl.semaphore_signal(barrier, inc=1, device_id=(a, r + 1), device_id_type=MESH)

    @pl.when(has_before == 1)
    def _():
        pl.semaphore_signal(barrier, inc=1, device_id=(a, r - 1), device_id_type=MESH)

    for j in (1, 2, 3):
        pl.semaphore_signal(barrier, inc=1, device_id=(2 * chip(j) + k, r), device_id_type=MESH)
    pl.semaphore_signal(barrier, inc=1, device_id=(peer, r), device_id_type=MESH)

    @pl.when(has_next == 0)
    def _():
        below[...] = jnp.zeros_like(below)

    @pl.when(has_before == 0)
    def _():
        above[...] = jnp.zeros_like(above)

    for ref in (own, above, below):
        rows = ref.shape[0]
        ref[:, 0:LANES] = jnp.zeros((rows, LANES), jnp.bfloat16)
        ref[:, LANES + wide :] = jnp.zeros((rows, LANES), jnp.bfloat16)
    stat_plain[...] = jnp.ones_like(stat_plain)
    stat_row[...] = jnp.zeros_like(stat_row)
    for copy in small:
        copy.wait()
    me_row = jnp.full((1, LANES), anchor[0, 0, 0], jnp.float32)
    me_col = jnp.full((1, LANES), anchor[0, 0, 1], jnp.float32)
    anchors[k, y] = jnp.concatenate([me_row, me_col, jnp.zeros((6, LANES), jnp.float32)], axis=0)

    pl.semaphore_wait(barrier, CHIPS + has_next + has_before)

    def anchor_copy(j):
        mine = anchors.at[k, y]
        return remote(mine, mine, anchor_send.at[j], anchor_recv.at[j], 2 * chip(j) + k, r)

    def anchor_share(parity):
        group = anchors.at[parity]
        return remote(group, group, anchor_send.at[0], anchor_recv.at[0], peer, r)

    first = 2 * chip(1) + k

    def halo_copy(m, side):
        at = (first + sign * (m - 1) + SECTIONS) % SECTIONS
        source = pl.ds(pl.multiple_of(at * PATCH, PATCH), PATCH)
        target = pl.ds(pl.multiple_of(at * PATCH + LANES, LANES), PATCH)
        rows, ref, to = ((PATCH - MARGIN, above, r + 1), (0, below, r - 1))[side]
        return remote(
            x_ref.at[0, pl.ds(rows, MARGIN), source],
            ref.at[:, target],
            halo_send.at[side, m],
            halo_recv.at[side, m],
            a,
            to,
        )

    def each_halo(sending, act):
        for side in (0, 1):
            there = has_next if (side == 0) == sending else has_before

            @pl.when(there == 1)
            def _():
                act(side)

    for j in (1, 2, 3):
        anchor_copy(j).start()

    def start_halos(side):
        for m in range(SECTIONS):
            halo_copy(m, side).start()

    each_halo(True, start_halos)

    def wait_halos(steps):
        def wait(side):
            for m in steps:
                halo_copy(m, side).wait_recv()

        each_halo(False, wait)

    local_own.wait()
    local_table.wait()
    for j in (1, 2, 3):
        anchor_copy(j).wait_recv()
    anchor_share(k).start()

    def cut(c, parity):
        base = pl.multiple_of(c * PATCH + LANES, LANES)
        shift_row = anchors[parity, c // 2, 0:1, :]
        shift_col = anchors[parity, c // 2, 1:2, :]
        sub = lax.broadcasted_iota(jnp.int32, (MARGIN, LANES), 0).astype(jnp.float32)
        lane = lax.broadcasted_iota(jnp.int32, (16, LANES), 1).astype(jnp.float32)

        def mask(condition):
            one = jnp.where(condition, 1.0, 0.0)
            return one.astype(jnp.bfloat16), (1.0 - one).astype(jnp.bfloat16)

        from_below, not_below = mask(sub < shift_row)
        from_above, not_above = mask(sub >= shift_row + MARGIN)
        from_right, not_right = mask(lane < shift_col)
        from_left, not_left = mask(lane >= shift_col + LANES)

        def rows_of(offset):
            lanes = pl.ds(pl.multiple_of(base + offset, LANES), LANES)
            top = below[:, lanes] * from_below + own[0:MARGIN, lanes] * not_below
            middle = own[MARGIN : PATCH - MARGIN, lanes]
            bottom = above[:, lanes] * from_above + own[PATCH - MARGIN :, lanes] * not_above
            return jnp.concatenate([top, middle, bottom], axis=0).reshape(PATCH // 16, 16, LANES)

        left = rows_of(PATCH) * from_right[None] + rows_of(0) * not_right[None]
        right = rows_of(-LANES) * from_left[None] + rows_of(LANES) * not_left[None]
        return jnp.concatenate([left.reshape(PATCH, LANES), right.reshape(PATCH, LANES)], axis=1)

    head8 = lax.broadcasted_iota(jnp.int32, (8, PATCH), 0) == 0
    zero8 = jnp.zeros((8, PATCH), jnp.float32)

    def analyse(c, parity):
        values = cut(c, parity)
        rows = dot(table[2], values)
        mean = jnp.sum(rows[0:1, :], axis=1, keepdims=True) * (1.0 / (PATCH * PATCH))
        centred = values.astype(jnp.float32) - mean
        squares = jnp.sum((centred * centred).reshape(PATCH // 8, 8, PATCH), axis=0)
        squares = jnp.sum(jnp.sum(squares, axis=0, keepdims=True), axis=1, keepdims=True)
        scale = lax.rsqrt(squares * (1.0 / (PATCH * PATCH)) + 1e-05)
        top = rows[:8] - jnp.where(head8, mean * float(PATCH), zero8)
        return jnp.concatenate([top, rows[8:]], axis=0).astype(jnp.bfloat16), scale

    def transform(rows, scale, target):
        by_cos = dot(rows, table[0])
        by_sin = dot(rows, table[1])
        real = by_cos[8:HALF] + by_sin[HALF + 8 :]
        imag = by_cos[HALF + 8 :] - by_sin[8:HALF]
        cos_last, sin_last = by_cos[HALF : HALF + 8], by_sin[HALF : HALF + 8]
        real8 = by_cos[:8] + jnp.where(head8, zero8, sin_last)
        imag8 = jnp.where(head8, zero8, cos_last) - by_sin[:8]
        last = jnp.concatenate([jnp.where(head8, cos_last, zero8), jnp.where(head8, -sin_last, zero8)], axis=0)
        whole = jnp.concatenate([real8, real, imag8, imag, last], axis=0)
        target[...] = (whole * scale).astype(jnp.bfloat16)

    def direct(j):
        return remote(send.at[j], spec.at[a], spec_send.at[j], spec_recv.at[a], 2 * chip(j + 1) + k, r)

    def hand(j):
        target = passing.at[j] if j < 3 else spec.at[a]
        received = passing_recv.at[j] if j < 3 else spec_recv.at[a]
        return remote(send.at[3 + j], target, spec_send.at[3 + j], received, peer, r)

    def forward(j):
        to = 2 * chip(-(j + 1)) + k
        return remote(passing.at[j], spec.at[peer], passing_send.at[j], spec_recv.at[peer], to, r)

    for j, steps in enumerate(((0, 1, 2), (3, 4), (5, 6), (7,))):
        wait_halos(steps)
        rows, scale = analyse(2 * chip(j + 1) + k, k)
        transform(rows, scale, send.at[j] if j < 3 else spec.at[a])
        if j < 3:
            direct(j).start()

    anchor_share(1 - k).wait_recv()
    ahead = analyse(2 * chip(1) + 1 - k, 1 - k)
    for j in range(4):
        now = ahead
        if j < 3:
            ahead = analyse(2 * chip(j + 2) + 1 - k, 1 - k)
        transform(*now, send.at[3 + j])
        hand(j).start()
        if j > 0:
            hand(j - 1).wait_recv()
            forward(j - 1).start()

    def cross(s, t):
        def part(section, start, stop):
            return spec[section, start:stop, :].astype(jnp.float32)

        def products(a_re, a_im, b_re, b_im):
            return a_re * b_re + a_im * b_im, a_re * b_im - a_im * b_re

        real, imag = products(part(s, 0, HALF), part(s, HALF, PATCH), part(t, 0, HALF), part(t, HALF, PATCH))
        e, f = part(s, PATCH, PATCH + EXTRA), part(t, PATCH, PATCH + EXTRA)
        last_re, last_im = products(e[:8], e[8:], f[:8], f[8:])
        return jnp.concatenate([real[:8] - last_im, real[8:], imag[:8] + last_re, imag[8:]], axis=0).astype(jnp.bfloat16)

    scale = BETA / math.log(2.0) / float(PATCH) ** 4
    group = lax.broadcasted_iota(jnp.int32, (PATCH // 8, 8, PATCH), 0).astype(jnp.float32) * 8.0
    signed_group = jnp.where(group < HALF, group, group - PATCH)

    def correlate(n):
        s = n // 2
        pair = cross(s, s + 1 + n % 2)
        by_cos = dot(pair, table[0])
        by_sin = dot(pair, table[1])
        half_re = by_cos[:HALF] - by_sin[HALF:]
        half_im = by_sin[:HALF] + by_cos[HALF:]
        half = jnp.concatenate([half_re, half_im], axis=0).astype(jnp.bfloat16)
        weight = jnp.exp2(dot(table[3], half) * scale).reshape(PATCH // 8, 8, PATCH)
        slot = s + SECTIONS * (n % 2)
        stat_plain[slot] = jnp.sum(weight, axis=0)
        stat_row[slot] = jnp.sum(weight * signed_group, axis=0)

    waits, work = plan()
    for q in range(SECTIONS):
        if q > 0:
            s = pick(waits[q], a)
            remote(send.at[0], spec.at[s], spec_send.at[0], spec_recv.at[s], peer, r).wait_recv()
        for entry in work[q]:
            correlate(pick(entry, a))

    plain = stat_plain[...]
    sub = lax.broadcasted_iota(jnp.int32, plain.shape, 1).astype(jnp.float32)
    by_row = jnp.sum(stat_row[...] + sub * plain, axis=1)
    plain = jnp.sum(plain, axis=1)
    column = lax.broadcasted_iota(jnp.int32, plain.shape, 1).astype(jnp.float32)
    signed = jnp.where(column < HALF, column, column - PATCH)
    total = jnp.sum(plain, axis=1, keepdims=True)
    shift_row = jnp.sum(by_row, axis=1, keepdims=True) / total / SHIFT_UNIT
    shift_col = jnp.sum(plain * signed, axis=1, keepdims=True) / total / SHIFT_UNIT
    lane = lax.broadcasted_iota(jnp.int32, (SECTIONS, LANES), 1)
    section = lax.broadcasted_iota(jnp.int32, (SECTIONS, LANES), 0)
    lanes = lax.broadcasted_iota(jnp.int32, (1, LANES), 1)
    for lag in (1, 2):
        keep = jnp.zeros((1, LANES), jnp.float32)
        for s in range(SECTIONS - lag):
            both = (1 - missing[s]) * (1 - missing[s + lag]) * valid[0, 0]
            keep = jnp.where(lanes == s, both.astype(jnp.float32), keep)
        for axis, shift in enumerate((shift_row, shift_col)):
            part = shift[(lag - 1) * SECTIONS : lag * SECTIONS]
            line = jnp.sum(jnp.where(lane == section, part, 0.0), axis=0, keepdims=True) * keep
            out_ref[axis, lag - 1] = line.reshape(1, 1, LANES)[:, :, :SECTIONS]

    def sent_halos(side):
        for m in range(SECTIONS):
            halo_copy(m, side).wait_send()

    each_halo(True, sent_halos)
    for j in (1, 2, 3):
        anchor_copy(j).wait_send()
        direct(j - 1).wait_send()
        forward(j - 1).wait_send()
    anchor_share(k).wait_send()
    for j in range(4):
        hand(j).wait_send()


def body(row_count, sections_img, missing, patch_anchor, block_valid):
    wide = SECTIONS * PATCH
    bf16, f32, i32 = jnp.bfloat16, jnp.float32, jnp.int32
    dma = pltpu.SemaphoreType.DMA
    flow = pl.pallas_call(
        functools.partial(kernel, row_count),
        out_shape=jax.ShapeDtypeStruct((2, 2, 1, 1, SECTIONS), f32),
        in_specs=[pl.BlockSpec(memory_space=pl.ANY)] * 5,
        out_specs=pl.BlockSpec(memory_space=pltpu.VMEM),
        scratch_shapes=[
            pltpu.SMEM((1, 1, 2), i32),
            pltpu.SMEM((SECTIONS,), i32),
            pltpu.SMEM((1, 1), i32),
            pltpu.VMEM((PATCH, wide + 2 * LANES), bf16),
            pltpu.VMEM((MARGIN, wide + 2 * LANES), bf16),
            pltpu.VMEM((MARGIN, wide + 2 * LANES), bf16),
            pltpu.VMEM((4, PATCH, PATCH), bf16),
            pltpu.VMEM((2, CHIPS, 8, LANES), f32),
            pltpu.VMEM((7, PATCH + EXTRA, PATCH), bf16),
            pltpu.VMEM((3, PATCH + EXTRA, PATCH), bf16),
            pltpu.VMEM((SECTIONS, PATCH + EXTRA, PATCH), bf16),
            pltpu.VMEM((2 * SECTIONS, 8, PATCH), f32),
            pltpu.VMEM((2 * SECTIONS, 8, PATCH), f32),
            dma((5,)),
            dma((2, SECTIONS)),
            dma((2, SECTIONS)),
            dma((CHIPS,)),
            dma((CHIPS,)),
            dma((7,)),
            dma((SECTIONS,)),
            dma((3,)),
            dma((3,)),
        ],
        compiler_params=pltpu.CompilerParams(
            collective_id=0, has_side_effects=True, vmem_limit_bytes=60 * 2**20
        ),
        name="flow",
    )(sections_img, jnp.transpose(patch_anchor, (1, 2, 0)), missing, block_valid, jnp.asarray(tables()))
    return jnp.transpose(flow, (0, 1, 4, 2, 3))


def solution(mesh):
    placed = (P("sec", "xy", None), P(), P(None, "xy", "sec"), P("xy", "sec"))
    return jax.shard_map(
        functools.partial(body, mesh.shape["xy"]),
        mesh=mesh,
        in_specs=placed,
        out_specs=P(None, None, None, "xy", "sec"),
        check_vma=False,
    )
```

time: 112 us -> 31.7 us (0.28)
  the two profiles are of different devices: /device:TPU:168 before, /device:TPU:129 now
where the time goes in v2:
time: 31.7 us; the launch traced here: 31.6 us
  Pallas kernels  29.7 us (94%)
  local copies, waits for them, and re-layouts  1.26 us (4%)
  between operations  0.66 us (2%)
    pallas_call x1, Pallas kernels, body(): pl.pallas_call(functools.partial(kernel, row_count), out_shape=jax.ShapeD...  29.7 us
    unnamed x1, local copies, waits for them, and re-layouts  1.26 us

profile of v2, /device:TPU:129, one launch (start us, length us, event | category | flops | bytes accessed | tf_op | source)
XLA Modules:
  0.0 31.6 jit_solution(6952393007358956876)
XLA Ops:
  0.7 29.7 %flow.1 = f32[2,2,1,1,8]{4,3,2,1,0:T(1,128)} custom-call(bf16[1,256,2048]{2,1,0:T(8,128)(2,1)} %x_ref.1, s32[1,1,2]{2,1,0:T(1,128)} %bitcast.5, s32[8]{0:T(128)} %missing_ref.1, s32[1,1]{1,0:T(1,128)S(6)} %copy.8.valid_ref, bf16[4,256,256]{2,1,0:T(8,128)(2,1)} %constant.2.clone.table_ref), custom_call_target="tpu_custom_call" | custom-call | tf_op jit(solution)/shard_map/flow/pallas_call | solution.py:382
  30.4 1.3 %copy.9 = f32[2,2,8,1,1]{2,4,3,1,0:T(1,128)} copy(f32[2,2,8,1,1]{2,4,3,1,0:T(1,128)} %bitcast.4) | data formatting | bytes 256

commit v3 on v2

--- a/solution.py
+++ b/solution.py
@@ -16,6 +16,7 @@
 EXTRA = 16
 SECTIONS = 8
 CHIPS = 4
+BATCH = 2
 BETA = 30.0
 SHIFT_UNIT = 8.0
 MESH = pl.DeviceIdType.MESH
@@ -138,7 +139,7 @@
     def _():
         pl.semaphore_signal(barrier, inc=1, device_id=(a, r - 1), device_id_type=MESH)
 
-    for j in (1, 2, 3):
+    for j in (1, -1):
         pl.semaphore_signal(barrier, inc=1, device_id=(2 * chip(j) + k, r), device_id_type=MESH)
     pl.semaphore_signal(barrier, inc=1, device_id=(peer, r), device_id_type=MESH)
 
@@ -150,10 +151,8 @@
     def _():
         above[...] = jnp.zeros_like(above)
 
-    for ref in (own, above, below):
-        rows = ref.shape[0]
-        ref[:, 0:LANES] = jnp.zeros((rows, LANES), jnp.bfloat16)
-        ref[:, LANES + wide :] = jnp.zeros((rows, LANES), jnp.bfloat16)
+    own[:, 0:LANES] = jnp.zeros((PATCH, LANES), jnp.bfloat16)
+    own[:, LANES + wide :] = jnp.zeros((PATCH, LANES), jnp.bfloat16)
     stat_plain[...] = jnp.ones_like(stat_plain)
     stat_row[...] = jnp.zeros_like(stat_row)
     for copy in small:
@@ -162,26 +161,27 @@
     me_col = jnp.full((1, LANES), anchor[0, 0, 1], jnp.float32)
     anchors[k, y] = jnp.concatenate([me_row, me_col, jnp.zeros((6, LANES), jnp.float32)], axis=0)
 
-    pl.semaphore_wait(barrier, CHIPS + has_next + has_before)
-
-    def anchor_copy(j):
-        mine = anchors.at[k, y]
-        return remote(mine, mine, anchor_send.at[j], anchor_recv.at[j], 2 * chip(j) + k, r)
+    local_own.wait()
+    pl.semaphore_wait(barrier, 3 + has_next + has_before)
+
+    def anchor_copy(i):
+        moved, to = ((y, 1), (y, -1), (chip(1), -1))[i]
+        group = anchors.at[k, moved]
+        return remote(group, group, anchor_send.at[i], anchor_recv.at[i], 2 * chip(to) + k, r)
 
     def anchor_share(parity):
         group = anchors.at[parity]
-        return remote(group, group, anchor_send.at[0], anchor_recv.at[0], peer, r)
-
-    first = 2 * chip(1) + k
+        return remote(group, group, anchor_send.at[3], anchor_recv.at[3], peer, r)
 
     def halo_copy(m, side):
-        at = (first + sign * (m - 1) + SECTIONS) % SECTIONS
-        source = pl.ds(pl.multiple_of(at * PATCH, PATCH), PATCH)
-        target = pl.ds(pl.multiple_of(at * PATCH + LANES, LANES), PATCH)
+        if m < CHIPS:
+            columns = pl.ds(pl.multiple_of((2 * chip(m + 1) + k) * PATCH, PATCH), 2 * PATCH)
+        else:
+            columns = pl.ds(pl.multiple_of((1 - k) * wide, PATCH), PATCH)
         rows, ref, to = ((PATCH - MARGIN, above, r + 1), (0, below, r - 1))[side]
         return remote(
-            x_ref.at[0, pl.ds(rows, MARGIN), source],
-            ref.at[:, target],
+            own.at[pl.ds(rows, MARGIN), columns],
+            ref.at[:, columns],
             halo_send.at[side, m],
             halo_recv.at[side, m],
             a,
@@ -196,27 +196,21 @@
             def _():
                 act(side)
 
-    for j in (1, 2, 3):
-        anchor_copy(j).start()
-
-    def start_halos(side):
-        for m in range(SECTIONS):
-            halo_copy(m, side).start()
-
-    each_halo(True, start_halos)
-
-    def wait_halos(steps):
-        def wait(side):
-            for m in steps:
-                halo_copy(m, side).wait_recv()
-
-        each_halo(False, wait)
-
-    local_own.wait()
+    anchor_copy(1).start()
+    anchor_copy(0).start()
+
+    def start_halo(m):
+        each_halo(True, lambda side: halo_copy(m, side).start())
+
+    def wait_halo(m):
+        each_halo(False, lambda side: halo_copy(m, side).wait_recv())
+
+    for m in range(CHIPS + 1):
+        start_halo(m)
+
+    anchor_copy(1).wait_recv()
+    anchor_copy(2).start()
     local_table.wait()
-    for j in (1, 2, 3):
-        anchor_copy(j).wait_recv()
-    anchor_share(k).start()
 
     def cut(c, parity):
         base = pl.multiple_of(c * PATCH + LANES, LANES)
@@ -283,14 +277,19 @@
         to = 2 * chip(-(j + 1)) + k
         return remote(passing.at[j], spec.at[peer], passing_send.at[j], spec_recv.at[peer], to, r)
 
-    for j, steps in enumerate(((0, 1, 2), (3, 4), (5, 6), (7,))):
-        wait_halos(steps)
+    for j in range(4):
+        wait_halo(j)
         rows, scale = analyse(2 * chip(j + 1) + k, k)
         transform(rows, scale, send.at[j] if j < 3 else spec.at[a])
         if j < 3:
             direct(j).start()
+        if j == 0:
+            anchor_copy(2).wait_recv()
+            anchor_copy(0).wait_recv()
+            anchor_share(k).start()
 
     anchor_share(1 - k).wait_recv()
+    wait_halo(4)
     ahead = analyse(2 * chip(1) + 1 - k, 1 - k)
     for j in range(4):
         now = ahead
@@ -318,26 +317,28 @@
     group = lax.broadcasted_iota(jnp.int32, (PATCH // 8, 8, PATCH), 0).astype(jnp.float32) * 8.0
     signed_group = jnp.where(group < HALF, group, group - PATCH)
 
-    def correlate(n):
-        s = n // 2
-        pair = cross(s, s + 1 + n % 2)
-        by_cos = dot(pair, table[0])
-        by_sin = dot(pair, table[1])
-        half_re = by_cos[:HALF] - by_sin[HALF:]
-        half_im = by_sin[:HALF] + by_cos[HALF:]
-        half = jnp.concatenate([half_re, half_im], axis=0).astype(jnp.bfloat16)
-        weight = jnp.exp2(dot(table[3], half) * scale).reshape(PATCH // 8, 8, PATCH)
-        slot = s + SECTIONS * (n % 2)
-        stat_plain[slot] = jnp.sum(weight, axis=0)
-        stat_row[slot] = jnp.sum(weight * signed_group, axis=0)
+    def correlate(numbers):
+        crosses = [cross(n // 2, n // 2 + 1 + n % 2) for n in numbers]
+        by_cos = [dot(pair, table[0]) for pair in crosses]
+        by_sin = [dot(pair, table[1]) for pair in crosses]
+        halves = []
+        for c, s in zip(by_cos, by_sin):
+            half = jnp.concatenate([c[:HALF] - s[HALF:], s[:HALF] + c[HALF:]], axis=0)
+            halves.append(half.astype(jnp.bfloat16))
+        full = [dot(table[3], half) for half in halves]
+        for n, corr in zip(numbers, full):
+            weight = jnp.exp2(corr * scale).reshape(PATCH // 8, 8, PATCH)
+            slot = n // 2 + SECTIONS * (n % 2)
+            stat_plain[slot] = jnp.sum(weight, axis=0)
+            stat_row[slot] = jnp.sum(weight * signed_group, axis=0)
 
     waits, work = plan()
     for q in range(SECTIONS):
         if q > 0:
             s = pick(waits[q], a)
             remote(send.at[0], spec.at[s], spec_send.at[0], spec_recv.at[s], peer, r).wait_recv()
-        for entry in work[q]:
-            correlate(pick(entry, a))
+        for i in range(0, len(work[q]), BATCH):
+            correlate([pick(entry, a) for entry in work[q][i : i + BATCH]])
 
     plain = stat_plain[...]
     sub = lax.broadcasted_iota(jnp.int32, plain.shape, 1).astype(jnp.float32)
@@ -361,15 +362,12 @@
             line = jnp.sum(jnp.where(lane == section, part, 0.0), axis=0, keepdims=True) * keep
             out_ref[axis, lag - 1] = line.reshape(1, 1, LANES)[:, :, :SECTIONS]
 
-    def sent_halos(side):
-        for m in range(SECTIONS):
-            halo_copy(m, side).wait_send()
-
-    each_halo(True, sent_halos)
-    for j in (1, 2, 3):
+    for m in range(CHIPS + 1):
+        each_halo(True, lambda side: halo_copy(m, side).wait_send())
+    for j in range(3):
         anchor_copy(j).wait_send()
-        direct(j - 1).wait_send()
-        forward(j - 1).wait_send()
+        direct(j).wait_send()
+        forward(j).wait_send()
     anchor_share(k).wait_send()
     for j in range(4):
         hand(j).wait_send()
@@ -382,7 +380,7 @@
     flow = pl.pallas_call(
         functools.partial(kernel, row_count),
         out_shape=jax.ShapeDtypeStruct((2, 2, 1, 1, SECTIONS), f32),
-        in_specs=[pl.BlockSpec(memory_space=pl.ANY)] * 5,
+        in_specs=[pl.BlockSpec(memory_space=pltpu.HBM)] * 5,
         out_specs=pl.BlockSpec(memory_space=pltpu.VMEM),
         scratch_shapes=[
             pltpu.SMEM((1, 1, 2), i32),
@@ -399,8 +397,8 @@
             pltpu.VMEM((2 * SECTIONS, 8, PATCH), f32),
             pltpu.VMEM((2 * SECTIONS, 8, PATCH), f32),
             dma((5,)),
-            dma((2, SECTIONS)),
-            dma((2, SECTIONS)),
+            dma((2, CHIPS + 1)),
+            dma((2, CHIPS + 1)),
             dma((CHIPS,)),
             dma((CHIPS,)),
             dma((7,)),
@@ -409,7 +407,7 @@
             dma((3,)),
         ],
         compiler_params=pltpu.CompilerParams(
-            collective_id=0, has_side_effects=True, vmem_limit_bytes=60 * 2**20
+            collective_id=0, has_side_effects=True, vmem_limit_bytes=55000 * 1024
         ),
         name="flow",
     )(sections_img, jnp.transpose(patch_anchor, (1, 2, 0)), missing, block_valid, jnp.asarray(tables()))

time: 31.7 us -> 28.6 us (0.902)
  Pallas kernels: 29.7 us -> 26.6 us
    pallas_call x1, Pallas kernels: 29.7 us -> 26.6 us  [body(): pl.pallas_call(functools.partial(kernel, row_count), out_shape=jax.ShapeD...]
    unnamed x1 -> x5, local copies, waits for them, and re-layouts: 1.26 us -> 1.24 us
where the time goes in v3:
time: 28.6 us; the launch traced here: 28.5 us
  Pallas kernels  26.6 us (93%)
  local copies, waits for them, and re-layouts  1.24 us (4%)
  between operations  0.68 us (2%)
    pallas_call x1, Pallas kernels, body(): pl.pallas_call(functools.partial(kernel, row_count), out_shape=jax.ShapeD...  26.6 us
    unnamed x5, local copies, waits for them, and re-layouts  1.24 us

profile of v3, /device:TPU:129, one launch (start us, length us, event | category | flops | bytes accessed | tf_op | source)
XLA Modules:
  0.0 28.5 jit_solution(246802519369394893)
XLA Ops:
  0.7 0.0 copy-start
  0.7 0.0 copy-start.1
  0.7 0.6 %copy-done = s32[2,1,1]{0,2,1:T(1,128)S(1)} copy-done((s32[2,1,1]{0,2,1:T(1,128)S(1)}, s32[2,1,1]{0,2,1:T(1,128)}, u32[]{:S(2)}) %copy-start) | copy-done | bytes 32
  1.3 0.0 copy-done.1
  1.3 26.6 %flow.1 = f32[2,2,1,1,8]{4,3,2,1,0:T(1,128)S(1)} custom-call(bf16[1,256,2048]{2,1,0:T(8,128)(2,1)} %x_ref.1, s32[1,1,2]{2,1,0:T(1,128)S(1)} %bitcast.5, s32[8]{0:T(128)S(1)} %copy-done.1, s32[1,1]{1,0:T(1,128)S(6)} %copy.8.valid_ref, bf16[4,256,256]{2,1,0:T(8,128)(2,1)} %constant.2.clone.table_ref), custom_call_target="tpu_custom_call" | custom-call | tf_op jit(solution)/shard_map/flow/pallas_call | solution.py:380
  27.9 0.6 %copy.9 = f32[2,2,8,1,1]{2,4,3,1,0:T(1,128)} copy(f32[2,2,8,1,1]{2,4,3,1,0:T(1,128)S(1)} %bitcast.4) | data formatting | bytes 256
Async XLA Ops:
  0.7 0.7 %copy-start = (s32[2,1,1]{0,2,1:T(1,128)S(1)}, s32[2,1,1]{0,2,1:T(1,128)}, u32[]{:S(2)}) copy-start(s32[2,1,1]{0,2,1:T(1,128)} %param.7) | copy-start | bytes 28
  0.7 0.7 %copy-start.1 = (s32[8]{0:T(128)S(1)}, s32[8]{0:T(128)}, u32[]{:S(2)}) copy-start(s32[8]{0:T(128)} %missing_ref.1) | copy-start | bytes 100

commit v4 on v3

--- a/solution.py
+++ b/solution.py
@@ -13,10 +13,9 @@
 HALF = PATCH // 2
 MARGIN = 64
 LANES = 128
-EXTRA = 16
 SECTIONS = 8
 CHIPS = 4
-BATCH = 2
+BATCH = 4
 BETA = 30.0
 SHIFT_UNIT = 8.0
 MESH = pl.DeviceIdType.MESH
@@ -241,6 +240,8 @@
 
     head8 = lax.broadcasted_iota(jnp.int32, (8, PATCH), 0) == 0
     zero8 = jnp.zeros((8, PATCH), jnp.float32)
+    lane8 = lax.broadcasted_iota(jnp.int32, (8, HALF), 1)
+    mirror8 = (HALF - lane8) % HALF
 
     def analyse(c, parity):
         values = cut(c, parity)
@@ -258,11 +259,15 @@
         by_sin = dot(rows, table[1])
         real = by_cos[8:HALF] + by_sin[HALF + 8 :]
         imag = by_cos[HALF + 8 :] - by_sin[8:HALF]
-        cos_last, sin_last = by_cos[HALF : HALF + 8], by_sin[HALF : HALF + 8]
-        real8 = by_cos[:8] + jnp.where(head8, zero8, sin_last)
-        imag8 = jnp.where(head8, zero8, cos_last) - by_sin[:8]
-        last = jnp.concatenate([jnp.where(head8, cos_last, zero8), jnp.where(head8, -sin_last, zero8)], axis=0)
-        whole = jnp.concatenate([real8, real, imag8, imag, last], axis=0)
+        def mirrored(row):
+            re, im = by_cos[row : row + 8], -by_sin[row : row + 8]
+            return re[:, :HALF], jnp.where(lane8 == 0, re[:, HALF:], im[:, :HALF])
+
+        zero_re, zero_im = mirrored(0)
+        last_re, last_im = mirrored(HALF)
+        real8 = jnp.where(head8, jnp.concatenate([zero_re, last_re], axis=1), by_cos[:8] + by_sin[HALF : HALF + 8])
+        imag8 = jnp.where(head8, jnp.concatenate([zero_im, last_im], axis=1), by_cos[HALF : HALF + 8] - by_sin[:8])
+        whole = jnp.concatenate([real8, real, imag8, imag], axis=0)
         target[...] = (whole * scale).astype(jnp.bfloat16)
 
     def direct(j):
@@ -308,10 +313,25 @@
         def products(a_re, a_im, b_re, b_im):
             return a_re * b_re + a_im * b_im, a_re * b_im - a_im * b_re
 
-        real, imag = products(part(s, 0, HALF), part(s, HALF, PATCH), part(t, 0, HALF), part(t, HALF, PATCH))
-        e, f = part(s, PATCH, PATCH + EXTRA), part(t, PATCH, PATCH + EXTRA)
-        last_re, last_im = products(e[:8], e[8:], f[:8], f[8:])
-        return jnp.concatenate([real[:8] - last_im, real[8:], imag[:8] + last_re, imag[8:]], axis=0).astype(jnp.bfloat16)
+        a_re, a_im = part(s, 0, HALF), part(s, HALF, PATCH)
+        b_re, b_im = part(t, 0, HALF), part(t, HALF, PATCH)
+        real, imag = products(a_re, a_im, b_re, b_im)
+
+        def mirrored(side):
+            re, im = real[:8, side], imag[:8, side]
+            first_one = a_re[:8, side] * b_re[:8, side]
+            middle = a_im[:8, side] * b_im[:8, side]
+            return jnp.where(lane8 == 0, first_one, re), jnp.where(lane8 == 0, 0.0, im), middle
+
+        zero_re, zero_im, zero_mid = mirrored(slice(0, HALF))
+        last_re, last_im, last_mid = mirrored(slice(HALF, PATCH))
+        far_re = jnp.where(lane8 == 0, zero_mid, jnp.take_along_axis(zero_re + last_im, mirror8, axis=1))
+        far_im = jnp.where(lane8 == 0, last_mid, jnp.take_along_axis(last_re - zero_im, mirror8, axis=1))
+        real8 = jnp.concatenate([zero_re - last_im, far_re], axis=1)
+        imag8 = jnp.concatenate([zero_im + last_re, far_im], axis=1)
+        real8 = jnp.where(head8, real8, real[:8])
+        imag8 = jnp.where(head8, imag8, imag[:8])
+        return jnp.concatenate([real8, real[8:], imag8, imag[8:]], axis=0).astype(jnp.bfloat16)
 
     scale = BETA / math.log(2.0) / float(PATCH) ** 4
     group = lax.broadcasted_iota(jnp.int32, (PATCH // 8, 8, PATCH), 0).astype(jnp.float32) * 8.0
@@ -391,9 +411,9 @@
             pltpu.VMEM((MARGIN, wide + 2 * LANES), bf16),
             pltpu.VMEM((4, PATCH, PATCH), bf16),
             pltpu.VMEM((2, CHIPS, 8, LANES), f32),
-            pltpu.VMEM((7, PATCH + EXTRA, PATCH), bf16),
-            pltpu.VMEM((3, PATCH + EXTRA, PATCH), bf16),
-            pltpu.VMEM((SECTIONS, PATCH + EXTRA, PATCH), bf16),
+            pltpu.VMEM((7, PATCH, PATCH), bf16),
+            pltpu.VMEM((3, PATCH, PATCH), bf16),
+            pltpu.VMEM((SECTIONS, PATCH, PATCH), bf16),
             pltpu.VMEM((2 * SECTIONS, 8, PATCH), f32),
             pltpu.VMEM((2 * SECTIONS, 8, PATCH), f32),
             dma((5,)),

time: 28.6 us -> 27.9 us (0.976)
  Pallas kernels: 26.6 us -> 25.9 us
    pallas_call x1, Pallas kernels: 26.6 us -> 25.9 us  [body(): pl.pallas_call(functools.partial(kernel, row_count), out_shape=jax.ShapeD...]
where the time goes in v4:
time: 27.9 us; the launch traced here: 27.8 us
  Pallas kernels  25.9 us (93%)
  local copies, waits for them, and re-layouts  1.24 us (4%)
  between operations  0.68 us (2%)
    pallas_call x1, Pallas kernels, body(): pl.pallas_call(functools.partial(kernel, row_count), out_shape=jax.ShapeD...  25.9 us
    unnamed x5, local copies, waits for them, and re-layouts  1.24 us

profile of v4, /device:TPU:129, one launch (start us, length us, event | category | flops | bytes accessed | tf_op | source)
XLA Modules:
  0.0 27.8 jit_solution(12630093324088911940)
XLA Ops:
  0.7 0.0 copy-start
  0.7 0.0 copy-start.1
  0.7 0.6 %copy-done = s32[2,1,1]{0,2,1:T(1,128)S(1)} copy-done((s32[2,1,1]{0,2,1:T(1,128)S(1)}, s32[2,1,1]{0,2,1:T(1,128)}, u32[]{:S(2)}) %copy-start) | copy-done | bytes 32
  1.3 0.0 copy-done.1
  1.3 25.9 %flow.1 = f32[2,2,1,1,8]{4,3,2,1,0:T(1,128)S(1)} custom-call(bf16[1,256,2048]{2,1,0:T(8,128)(2,1)} %x_ref.1, s32[1,1,2]{2,1,0:T(1,128)S(1)} %bitcast.5, s32[8]{0:T(128)S(1)} %copy-done.1, s32[1,1]{1,0:T(1,128)S(6)} %copy.8.valid_ref, bf16[4,256,256]{2,1,0:T(8,128)(2,1)} %constant.2.clone.table_ref), custom_call_target="tpu_custom_call" | custom-call | tf_op jit(solution)/shard_map/flow/pallas_call | solution.py:400
  27.2 0.6 %copy.9 = f32[2,2,8,1,1]{2,4,3,1,0:T(1,128)} copy(f32[2,2,8,1,1]{2,4,3,1,0:T(1,128)S(1)} %bitcast.4) | data formatting | bytes 256
Async XLA Ops:
  0.7 0.7 %copy-start = (s32[2,1,1]{0,2,1:T(1,128)S(1)}, s32[2,1,1]{0,2,1:T(1,128)}, u32[]{:S(2)}) copy-start(s32[2,1,1]{0,2,1:T(1,128)} %param.7) | copy-start | bytes 28
  0.7 0.7 %copy-start.1 = (s32[8]{0:T(128)S(1)}, s32[8]{0:T(128)}, u32[]{:S(2)}) copy-start(s32[8]{0:T(128)} %missing_ref.1) | copy-start | bytes 100

commit v5 on v4

--- a/solution.py
+++ b/solution.py
@@ -152,6 +152,9 @@
 
     own[:, 0:LANES] = jnp.zeros((PATCH, LANES), jnp.bfloat16)
     own[:, LANES + wide :] = jnp.zeros((PATCH, LANES), jnp.bfloat16)
+    margin = pl.ds(pl.multiple_of((1 - k) * (wide + LANES), LANES), LANES)
+    above[:, margin] = jnp.zeros((MARGIN, LANES), jnp.bfloat16)
+    below[:, margin] = jnp.zeros((MARGIN, LANES), jnp.bfloat16)
     stat_plain[...] = jnp.ones_like(stat_plain)
     stat_row[...] = jnp.zeros_like(stat_row)
     for copy in small:
@@ -176,7 +179,7 @@
         if m < CHIPS:
             columns = pl.ds(pl.multiple_of((2 * chip(m + 1) + k) * PATCH, PATCH), 2 * PATCH)
         else:
-            columns = pl.ds(pl.multiple_of((1 - k) * wide, PATCH), PATCH)
+            columns = pl.ds(pl.multiple_of((1 - k) * wide + k * LANES, LANES), LANES)
         rows, ref, to = ((PATCH - MARGIN, above, r + 1), (0, below, r - 1))[side]
         return remote(
             own.at[pl.ds(rows, MARGIN), columns],

time: 27.9 us -> 27.8 us (level)
  no operation moved by 1% of the time
where the time goes in v5:
time: 27.8 us; the launch traced here: 27.6 us
  Pallas kernels  25.7 us (92%)
  local copies, waits for them, and re-layouts  1.24 us (4%)
  between operations  0.68 us (2%)
    pallas_call x1, Pallas kernels, body(): pl.pallas_call(functools.partial(kernel, row_count), out_shape=jax.ShapeD...  25.7 us
    unnamed x5, local copies, waits for them, and re-layouts  1.24 us

profile of v5, /device:TPU:129, one launch (start us, length us, event | category | flops | bytes accessed | tf_op | source)
XLA Modules:
  0.0 27.6 jit_solution(3818593449988306827)
XLA Ops:
  0.7 0.0 copy-start
  0.7 0.0 copy-start.1
  0.7 0.6 %copy-done = s32[2,1,1]{0,2,1:T(1,128)S(1)} copy-done((s32[2,1,1]{0,2,1:T(1,128)S(1)}, s32[2,1,1]{0,2,1:T(1,128)}, u32[]{:S(2)}) %copy-start) | copy-done | bytes 32
  1.3 0.0 copy-done.1
  1.3 25.7 %flow.1 = f32[2,2,1,1,8]{4,3,2,1,0:T(1,128)S(1)} custom-call(bf16[1,256,2048]{2,1,0:T(8,128)(2,1)} %x_ref.1, s32[1,1,2]{2,1,0:T(1,128)S(1)} %bitcast.5, s32[8]{0:T(128)S(1)} %copy-done.1, s32[1,1]{1,0:T(1,128)S(6)} %copy.8.valid_ref, bf16[4,256,256]{2,1,0:T(8,128)(2,1)} %constant.2.clone.table_ref), custom_call_target="tpu_custom_call" | custom-call | tf_op jit(solution)/shard_map/flow/pallas_call | solution.py:403
  27.1 0.6 %copy.9 = f32[2,2,8,1,1]{2,4,3,1,0:T(1,128)} copy(f32[2,2,8,1,1]{2,4,3,1,0:T(1,128)S(1)} %bitcast.4) | data formatting | bytes 256
Async XLA Ops:
  0.7 0.7 %copy-start = (s32[2,1,1]{0,2,1:T(1,128)S(1)}, s32[2,1,1]{0,2,1:T(1,128)}, u32[]{:S(2)}) copy-start(s32[2,1,1]{0,2,1:T(1,128)} %param.7) | copy-start | bytes 28
  0.7 0.7 %copy-start.1 = (s32[8]{0:T(128)S(1)}, s32[8]{0:T(128)}, u32[]{:S(2)}) copy-start(s32[8]{0:T(128)} %missing_ref.1) | copy-start | bytes 100

commit v6 on v5

--- a/solution.py
+++ b/solution.py
@@ -15,7 +15,7 @@
 LANES = 128
 SECTIONS = 8
 CHIPS = 4
-BATCH = 4
+BATCH = 13
 BETA = 30.0
 SHIFT_UNIT = 8.0
 MESH = pl.DeviceIdType.MESH

time: 27.8 us -> 27.8 us (level)
  no operation moved by 1% of the time
where the time goes in v6:
time: 27.8 us; the launch traced here: 27.6 us
  Pallas kernels  25.7 us (92%)
  local copies, waits for them, and re-layouts  1.24 us (4%)
  between operations  0.68 us (2%)
    pallas_call x1, Pallas kernels, body(): pl.pallas_call(functools.partial(kernel, row_count), out_shape=jax.ShapeD...  25.7 us
    unnamed x5, local copies, waits for them, and re-layouts  1.24 us

profile of v6, /device:TPU:129, one launch (start us, length us, event | category | flops | bytes accessed | tf_op | source)
XLA Modules:
  0.0 27.6 jit_solution(3818593449988306827)
XLA Ops:
  0.7 0.0 copy-start
  0.7 0.0 copy-start.1
  0.7 0.6 %copy-done = s32[2,1,1]{0,2,1:T(1,128)S(1)} copy-done((s32[2,1,1]{0,2,1:T(1,128)S(1)}, s32[2,1,1]{0,2,1:T(1,128)}, u32[]{:S(2)}) %copy-start) | copy-done | bytes 32
  1.3 0.0 copy-done.1
  1.3 25.7 %flow.1 = f32[2,2,1,1,8]{4,3,2,1,0:T(1,128)S(1)} custom-call(bf16[1,256,2048]{2,1,0:T(8,128)(2,1)} %x_ref.1, s32[1,1,2]{2,1,0:T(1,128)S(1)} %bitcast.5, s32[8]{0:T(128)S(1)} %copy-done.1, s32[1,1]{1,0:T(1,128)S(6)} %copy.8.valid_ref, bf16[4,256,256]{2,1,0:T(8,128)(2,1)} %constant.2.clone.table_ref), custom_call_target="tpu_custom_call" | custom-call | tf_op jit(solution)/shard_map/flow/pallas_call | solution.py:403
  27.1 0.6 %copy.9 = f32[2,2,8,1,1]{2,4,3,1,0:T(1,128)} copy(f32[2,2,8,1,1]{2,4,3,1,0:T(1,128)S(1)} %bitcast.4) | data formatting | bytes 256
Async XLA Ops:
  0.7 0.7 %copy-start = (s32[2,1,1]{0,2,1:T(1,128)S(1)}, s32[2,1,1]{0,2,1:T(1,128)}, u32[]{:S(2)}) copy-start(s32[2,1,1]{0,2,1:T(1,128)} %param.7) | copy-start | bytes 28
  0.7 0.7 %copy-start.1 = (s32[8]{0:T(128)S(1)}, s32[8]{0:T(128)}, u32[]{:S(2)}) copy-start(s32[8]{0:T(128)} %missing_ref.1) | copy-start | bytes 100
